TPU v7x, 256 devices: a whole 4x4x8 slice. The times are simulated.
256 devices in a mesh: head: 4 (over z_hi), ctx: 64 (over z_lo, y, x, core).
Axes of the slice: x: 4, y: 4, z: 8 (z_hi: 4, z_lo: 2; z = z_hi * 2 + z_lo), core: 2. Of those that a mesh axis runs over, the one named last changes fastest.
Arguments:
- query: bfloat16 [32768, 8192], P(('ctx', 'head')), may hold values from -6 to 6
- key: bfloat16 [32768, 1024], P(('ctx', 'head')), may hold values from -6 to 6
- value: bfloat16 [32768, 1024], P(('ctx', 'head')), may hold values from -6 to 6
- out: bfloat16 [32768, 8192], P(('ctx', 'head')), may hold values from -6 to 6
- dout: bfloat16 [32768, 8192], P(('ctx', 'head')), may hold values from -6 to 6
- lse: float32 [32768, 64], P('ctx', 'head'), may hold values from 3 to 6
- span_order: int32 [128], replicated, may hold values from 0 to 127, each once
Outputs:
- grad_query: bfloat16 [32768, 8192], P(('ctx', 'head'))
- grad_key: bfloat16 [32768, 1024], P(('ctx', 'head'))
- grad_value: bfloat16 [32768, 1024], P(('ctx', 'head'))
Inputs may be any that keep to these rules, and one draw needn't show every extreme that they name: `span_order`: each of the 128 spans appears once.
All inputs are finite; a program needn't handle non-finite values.
Results may differ from a plain program's by a relative error of at most 0.0052.
Values may be sent and summed in bfloat16 or wider, within the bound.
A program may use at most 128 MiB of HBM per device.

v0:
```python
import functools
import math

import jax
import jax.numpy as jnp
from jax import lax
from jax.experimental import pallas as pl
from jax.experimental.pallas import tpu as pltpu
from jax.sharding import PartitionSpec as P

HD = 128
RING = 4
LOG2E = math.log2(math.e)
FAR = 1e30
AHEAD = 2
LAGS = (1, 3, 5, 6, 8)
MESH = pl.DeviceIdType.MESH
NT = (((1,), (1,)), ((), ()))
NN = (((1,), (0,)), ((), ()))


def dot(a, b, dims):
    return lax.dot_general(a, b, dims, preferred_element_type=jnp.float32)


def kernel(
    groups, per, q_hbm, k_hbm, v_hbm, o_hbm, d_hbm, lse_hbm, span_ref,
    dq_buf, dk_buf, dv_buf,
    q_buf, d_buf, o_buf, lse_buf, lse_cut, lse_all, delta_all, bias_own,
    kv, grad, back_out, back_in, cut_out, cut_in, sum_out, sum_in,
    key_t, p_all, s_all, q_all, d_all,
    load_sem, kv_sem,
    lse_s, lse_r, own_s, own_r, fwd_s, fwd_r, ctx_s, ctx_r, back_s, back_r, cut_s, cut_r, sum_s, sum_r,
):
    rows = q_buf.shape[0]
    span = 2 * rows
    heads_in = lse_cut.shape[1]
    cycle = lax.axis_size("ctx")
    me = lax.axis_index("head")
    here = lax.axis_index("ctx")
    up, opp, dn = lax.rem(me + 1, RING), lax.rem(me + 2, RING), lax.rem(me + 3, RING)
    nx, pv = lax.rem(here + 1, cycle), lax.rem(here + cycle - 1, cycle)
    at_up, at_dn, at_opp = (up, here), (dn, here), (opp, here)
    at_nx, at_pv = (me, nx), (me, pv)
    scale = HD ** -0.5

    def lanes(g, width=HD):
        return pl.ds(pl.multiple_of(g * width, width), width)

    def load(i):
        src, dst = ((q_hbm, q_buf), (d_hbm, d_buf), (o_hbm, o_buf), (lse_hbm, lse_buf))[i]
        return pltpu.make_async_copy(src, dst, load_sem.at[i])

    def load_kv(which, g):
        src = (k_hbm, v_hbm)[which]
        return pltpu.make_async_copy(src.at[:, lanes(g)], kv.at[0, g, which, me], kv_sem.at[which, g])

    def remote(src, dst, s, r, to):
        return pltpu.make_async_remote_copy(
            src_ref=src, dst_ref=dst, send_sem=s, recv_sem=r, device_id=to, device_id_type=MESH
        )

    def send_lse(i):
        to, target = ((up, at_up), (dn, at_dn), (opp, at_opp))[i]
        return remote(lse_cut.at[to], lse_all.at[me], lse_s.at[i], lse_r.at[i], target)

    def take_lse(i):
        src = (dn, up, opp)[i]
        return remote(lse_cut.at[src], lse_all.at[src], lse_s.at[i], lse_r.at[i], at_up)

    def own(side, g, slot):
        block = kv.at[0, g, :, slot]
        return remote(block, block, own_s.at[side, g], own_r.at[side, g], (at_up, at_dn)[side])

    def fwd(side, g, slot):
        block = kv.at[0, g, side, slot]
        return remote(block, block, fwd_s.at[side, g], fwd_r.at[side, g], (at_up, at_dn)[side])

    def ctx(g):
        return remote(kv.at[0, g], kv.at[1, g], ctx_s.at[g], ctx_r.at[g], at_nx)

    def back(g):
        return remote(back_out.at[g], back_in.at[g], back_s.at[g], back_r.at[g], at_pv)

    half = cycle // 2
    is_last = lax.rem(here, half) == half - 1
    is_first = lax.rem(here, half) == 0
    side_last = lax.rem(me + jnp.where(here < half, RING - 1, 1), RING)
    side_first = lax.rem(me + jnp.where(here < half, RING - 1, 1), RING)
    at_nx_v = (jnp.where(is_last, side_last, me), nx)
    at_pv_v = (jnp.where(is_first, side_first, me), pv)

    def start_ctx(g):
        for which, to in ((0, at_nx), (1, at_nx_v)):
            remote(kv.at[0, g, which], kv.at[1, g, which], ctx_s.at[g], ctx_r.at[g], to).start()

    def start_back(g):
        for which, to in ((0, at_pv), (1, at_pv_v)):
            remote(back_out.at[g, which], back_in.at[g, which], back_s.at[g], back_r.at[g], to).start()

    def signal(target):
        pl.semaphore_signal(barrier, inc=1, device_id=target, device_id_type=MESH)

    def cut(side, g):
        return remote(
            cut_out.at[g, side], cut_in.at[g, side], cut_s.at[side, g], cut_r.at[side, g], (at_up, at_dn)[side]
        )

    def summed(side, g):
        return remote(
            sum_out.at[g, side], sum_in.at[g, side], sum_s.at[side, g], sum_r.at[side, g], (at_up, at_dn)[side]
        )

    def loop(lo, hi, body, unroll=1):
        def step(i, carry):
            body(i)
            return carry

        lax.fori_loop(lo, hi, step, 0, unroll=unroll)

    def start_kv(g):
        load_kv(0, g).start()
        load_kv(1, g).start()

    loop(0, groups, start_kv)
    for i in (3, 1, 2, 0):
        load(i).start()

    barrier = pltpu.get_barrier_semaphore()
    for target in (at_up, at_dn, at_opp, at_nx, at_pv, at_nx_v, at_pv_v):
        signal(target)

    span_q = span_ref[2 * here + me // 2]
    first_q = (me % 2) * rows
    row = lax.broadcasted_iota(jnp.int32, (span, 2 * rows), 0)
    lane = lax.broadcasted_iota(jnp.int32, (span, 2 * rows), 1)
    ahead = lax.rem(lane, rows) - row
    for a in range(2):
        least = (span_ref[2 * here + a] - span_q) * span - first_q
        bias_own[a] = jnp.where(ahead >= least, 0.0, FAR)
    bias_prev = [jnp.where(span_q > span_ref[2 * pv + a], 0.0, FAR) for a in range(2)]

    pl.semaphore_wait(barrier, 7)

    def send_own(g):
        load_kv(0, g).wait()
        load_kv(1, g).wait()
        own(0, g, me).start()
        own(1, g, me).start()

    loop(0, min(AHEAD, groups), send_own)

    load(3).wait()
    for h in range(RING):
        lse_cut[h] = lse_buf[:, h * rows : (h + 1) * rows]
    for i in range(3):
        send_lse(i).start()
    lse_all[me] = lse_cut[me]

    ones = jnp.ones((8, 2 * HD), jnp.bfloat16)

    def make_delta(h):
        prod = o_buf[:, lanes(h)].astype(jnp.float32) * d_buf[:, lanes(h)].astype(jnp.float32)
        high = prod.astype(jnp.bfloat16)
        low = (prod - high.astype(jnp.float32)).astype(jnp.bfloat16)
        delta_all[pl.ds(h, 1), :] = dot(ones, jnp.concatenate([high, low], axis=1), NT)[0:1]

    def prepare():
        load(1).wait()
        load(2).wait()
        loop(0, groups * per, make_delta, 8)
        load(0).wait()
        for i in range(3):
            take_lse(i).wait_recv()


    def compute(g):

        def rows_of(j):
            head = g * per + 2 * j
            q_one, d_one = q_buf[:, lanes(head // 2, 2 * HD)], d_buf[:, lanes(head // 2, 2 * HD)]
            q2 = jnp.concatenate([q_one[:, :HD], q_one[:, HD:]], axis=0)
            d2 = jnp.concatenate([d_one[:, :HD], d_one[:, HD:]], axis=0)
            owner, low = head // heads_in, lax.rem(head, heads_in)
            lse2 = jnp.concatenate(
                [lse_all[owner, pl.ds(low, 1), :], lse_all[owner, pl.ds(low + 1, 1), :]], axis=1
            ) * LOG2E
            delta2 = jnp.concatenate([delta_all[pl.ds(head, 1), :], delta_all[pl.ds(head + 1, 1), :]], axis=1)
            return head, q2, d2, lse2, delta2

        for b in range(2):
            key_t[b] = kv[b, g, 0].reshape(2 * span, HD).T

        def pair(j):
            head, q2, d2, lse2, delta2 = rows_of(j)
            q_t, d_t = q2.T, d2.T
            q_all[pl.ds(pl.multiple_of(j * 2 * rows, 2 * rows), 2 * rows), :] = q2
            d_all[pl.ds(pl.multiple_of(j * 2 * rows, 2 * rows), 2 * rows), :] = d2
            for b in range(2):
                for a in range(2):
                    key = kv[b, g, 0, 2 * a : 2 * a + 2].reshape(span, HD)
                    value = kv[b, g, 1, 2 * a : 2 * a + 2].reshape(span, HD)
                    scores = dot(key, q_t, NN) * (scale * LOG2E)
                    if b == 0:
                        scores = scores - lse2 - bias_own[a]
                    else:
                        scores = scores - (lse2 + bias_prev[a])
                    probs = jnp.exp2(scores)
                    grad_probs = dot(value, d_t, NN)
                    grad_scores = (probs * (grad_probs - delta2) * scale).astype(jnp.bfloat16)
                    p_all[b, a * span : (a + 1) * span, lanes(j, 2 * HD)] = probs.astype(jnp.bfloat16)
                    s_all[b, a * span : (a + 1) * span, lanes(j, 2 * HD)] = grad_scores

        loop(0, per // 2, pair, True)
        for b in range(2):
            grad[g, b, 0] = dot(s_all[b], q_all[...], NN).reshape(RING, rows, HD)
            grad[g, b, 1] = dot(p_all[b], d_all[...], NN).reshape(RING, rows, HD)
        dq_all = dot(key_t[0], s_all[0], NN) + dot(key_t[1], s_all[1], NN)
        dq_buf[:, lanes(g, per * HD)] = jnp.concatenate([dq_all[:, rows * x : rows * (x + 1)].T for x in range(per)], axis=1).astype(jnp.bfloat16)
        back_out[g] = grad[g, 1].astype(jnp.bfloat16)

    def total(g, which, slot):
        return grad[g, 0, which, slot] + back_in[g, which, slot].astype(jnp.float32)

    def stage(i, lag, work):
        @pl.when((i >= lag) & (i < groups + lag))
        def _():
            work(i - lag)

    def forward(g):
        own(0, g, dn).wait_recv()
        fwd(0, g, dn).start()
        own(1, g, up).wait_recv()
        fwd(1, g, up).start()

    def pass_on(g):
        fwd(0, g, opp).wait_recv()
        fwd(1, g, opp).wait_recv()
        start_ctx(g)

    def start_cut(g):
        back(g).wait_recv()
        cut_out[g, 0, 0] = total(g, 0, opp).astype(jnp.bfloat16)
        cut_out[g, 0, 1] = total(g, 1, up).astype(jnp.bfloat16)
        cut(0, g).start()
        cut_out[g, 1, 0] = total(g, 1, opp).astype(jnp.bfloat16)
        cut_out[g, 1, 1] = total(g, 0, dn).astype(jnp.bfloat16)
        cut(1, g).start()

    def start_sum(g):
        cut(0, g).wait_recv()
        sum_out[g, 0] = (total(g, 0, up) + cut_in[g, 0, 0].astype(jnp.float32)).astype(jnp.bfloat16)
        summed(0, g).start()
        cut(1, g).wait_recv()
        sum_out[g, 1] = (total(g, 1, dn) + cut_in[g, 1, 0].astype(jnp.float32)).astype(jnp.bfloat16)
        summed(1, g).start()

    def work(g):
        ctx(g).wait_recv()
        compute(g)
        start_back(g)

    def finish(g):
        summed(0, g).wait_recv()
        summed(1, g).wait_recv()
        for which, out in ((0, dk_buf), (1, dv_buf)):
            out[:, lanes(g)] = (
                total(g, which, me)
                + sum_in[g, which].astype(jnp.float32)
                + cut_in[g, 1 - which, 1].astype(jnp.float32)
            ).astype(jnp.bfloat16)

    def step(i):
        @pl.when(i < groups - AHEAD)
        def _():
            send_own(i + AHEAD)

        stage(i, 0, forward)
        stage(i, LAGS[0], pass_on)
        @pl.when(i == 1)
        def _():
            prepare()

        stage(i, LAGS[2], start_cut)
        stage(i, LAGS[3], start_sum)
        stage(i, LAGS[1], work)
        stage(i, LAGS[4], finish)

    loop(0, groups + LAGS[4], step)

    def drain(g):
        for side in range(2):
            own(side, g, me).wait_send()
            fwd(side, g, (dn, up)[side]).wait_send()
            cut(side, g).wait_send()
            summed(side, g).wait_send()
        ctx(g).wait_send()
        back(g).wait_send()

    loop(0, groups, drain)
    for i in range(3):
        send_lse(i).wait_send()


def body(query, key, value, out, dout, lse, span_order):
    rows, width = query.shape
    groups = key.shape[1] // HD
    per = width // key.shape[1]
    bf, f32 = jnp.bfloat16, jnp.float32
    dma = pltpu.SemaphoreType.DMA
    hbm = pl.BlockSpec(memory_space=pl.ANY)
    pairs = [dma((2, groups))] * 2
    ones = [dma((groups,))] * 2
    return pl.pallas_call(
        functools.partial(kernel, groups, per),
        out_shape=tuple(pltpu.VMEM(x.shape, bf) for x in (query, key, value)),
        in_specs=[hbm] * 6 + [pl.BlockSpec(memory_space=pltpu.SMEM)],
        out_specs=[pl.BlockSpec(memory_space=pltpu.VMEM)] * 3,
        scratch_shapes=[
            pltpu.VMEM(query.shape, bf),
            pltpu.VMEM(query.shape, bf),
            pltpu.VMEM(query.shape, bf),
            pltpu.VMEM(lse.shape[::-1], f32),
            pltpu.VMEM((RING, lse.shape[1], rows), f32),
            pltpu.VMEM((RING, lse.shape[1], rows), f32),
            pltpu.VMEM((groups * per, rows), f32),
            pltpu.VMEM((2, 2 * rows, 2 * rows), f32),
            pltpu.VMEM((2, groups, 2, RING, rows, HD), bf),
            pltpu.VMEM((groups, 2, 2, RING, rows, HD), f32),
            pltpu.VMEM((groups, 2, RING, rows, HD), bf),
            pltpu.VMEM((groups, 2, RING, rows, HD), bf),
            pltpu.VMEM((groups, 2, 2, rows, HD), bf),
            pltpu.VMEM((groups, 2, 2, rows, HD), bf),
            pltpu.VMEM((groups, 2, rows, HD), bf),
            pltpu.VMEM((groups, 2, rows, HD), bf),
            pltpu.VMEM((2, HD, RING * rows), bf),
            pltpu.VMEM((2, RING * rows, per * rows), bf),
            pltpu.VMEM((2, RING * rows, per * rows), bf),
            pltpu.VMEM((per * rows, HD), bf),
            pltpu.VMEM((per * rows, HD), bf),
            dma((4,)),
            dma((2, groups)),
            dma((3,)),
            dma((3,)),
            *pairs,
            *pairs,
            *ones,
            *ones,
            *pairs,
            *pairs,
        ],
        compiler_params=pltpu.CompilerParams(
            collective_id=0, has_side_effects=True, vmem_limit_bytes=56 * 1024 * 1024
        ),
        cost_estimate=pl.CostEstimate(
            flops=20 * rows * width * RING * rows, bytes_accessed=10 * rows * width, transcendentals=0
        ),
    )(query, key, value, out, dout, lse.T, span_order)


def solution(mesh):
    token = P(("ctx", "head"), None)
    return jax.shard_map(
        body,
        mesh=mesh,
        in_specs=(token, token, token, token, token, P("ctx", "head"), P()),
        out_specs=(token, token, token),
        check_vma=False,
    )
```

profile of v0, /device:TPU:63, one launch (start us, length us, event | category | flops | bytes accessed | tf_op | source)
XLA Modules:
  0.0 100.4 jit_solution(13379105853373191183)
XLA Ops:
  0.6 97.0 %shard_map.94 = (bf16[128,8192]{1,0:T(8,128)(2,1)S(1)}, bf16[128,1024]{1,0:T(8,128)(2,1)S(1)}, bf16[128,1024]{1,0:T(8,128)(2,1)S(1)}) custom-call(bf16[128,8192]{1,0:T(8,128)(2,1)} %q_hbm.1, bf16[128,1024]{1,0:T(8,128)(2,1)} %k_hbm.1, bf16[128,1024]{1,0:T(8,128)(2,1)} %v_hbm.1, bf16[128,8192]{1,0:T(8,128)(2,1)} %o_hbm.1, bf16[128,8192]{1,0:T(8,128)(2,1)} %d_hbm.1, ...), custom_call_target="tpu_custom_call" | custom-call | flops 10737418240 | bytes 10485760 | tf_op jit(solution)/shard_map/pallas_call | solution.py:314
  97.7 1.3 %copy.13 = bf16[128,8192]{1,0:T(8,128)(2,1)} copy(bf16[128,8192]{1,0:T(8,128)(2,1)S(1)} %get-tuple-element.3) | data formatting | bytes 4194304
  99.0 0.7 copy.14
  99.7 0.7 copy.15
where the time goes:
time: 100 us
  Pallas kernels  97 us (97%)
  local copies, waits for them, and re-layouts  2.73 us (3%)
    pallas_call x1, Pallas kernels, body(): pl.pallas_call(functools.partial(kernel, groups, per), out_shape=tuple((p...  97 us
    unnamed x3, local copies, waits for them, and re-layouts  2.73 us

commit v1 on v0

--- a/solution.py
+++ b/solution.py
@@ -13,7 +13,7 @@
 LOG2E = math.log2(math.e)
 FAR = 1e30
 AHEAD = 2
-LAGS = (1, 3, 5, 6, 8)
+LAGS = (1, 3, 5, 7, 9)
 MESH = pl.DeviceIdType.MESH
 NT = (((1,), (1,)), ((), ()))
 NN = (((1,), (0,)), ((), ()))
@@ -212,12 +212,18 @@
                     s_all[b, a * span : (a + 1) * span, lanes(j, 2 * HD)] = grad_scores
 
         loop(0, per // 2, pair, True)
-        for b in range(2):
+        def keys_of(b):
             grad[g, b, 0] = dot(s_all[b], q_all[...], NN).reshape(RING, rows, HD)
             grad[g, b, 1] = dot(p_all[b], d_all[...], NN).reshape(RING, rows, HD)
+
+        keys_of(1)
+        back_out[g] = grad[g, 1].astype(jnp.bfloat16)
+        start_back(g)
+        keys_of(0)
         dq_all = dot(key_t[0], s_all[0], NN) + dot(key_t[1], s_all[1], NN)
-        dq_buf[:, lanes(g, per * HD)] = jnp.concatenate([dq_all[:, rows * x : rows * (x + 1)].T for x in range(per)], axis=1).astype(jnp.bfloat16)
-        back_out[g] = grad[g, 1].astype(jnp.bfloat16)
+        dq_buf[:, lanes(g, per * HD)] = jnp.concatenate(
+            [dq_all[:, rows * x : rows * (x + 1)].T for x in range(per)], axis=1
+        ).astype(jnp.bfloat16)
 
     def total(g, which, slot):
         return grad[g, 0, which, slot] + back_in[g, which, slot].astype(jnp.float32)
@@ -258,7 +264,6 @@
     def work(g):
         ctx(g).wait_recv()
         compute(g)
-        start_back(g)
 
     def finish(g):
         summed(0, g).wait_recv()

time: 100 us -> 97.5 us (0.975)
  Pallas kernels: 97 us -> 94 us
    pallas_call x1, Pallas kernels: 97 us -> 94 us  [body(): pl.pallas_call(functools.partial(kernel, groups, per), out_shape=tuple((p...]
where the time goes in v1:
time: 97.5 us; the launch traced here: 97.4 us
  Pallas kernels  94 us (96%)
  local copies, waits for them, and re-layouts  2.73 us (3%)
    pallas_call x1, Pallas kernels, body(): pl.pallas_call(functools.partial(kernel, groups, per), out_shape=tuple((p...  94 us
    unnamed x3, local copies, waits for them, and re-layouts  2.73 us

profile of v1, /device:TPU:63, one launch (start us, length us, event | category | flops | bytes accessed | tf_op | source)
XLA Modules:
  0.0 97.4 jit_solution(16432180042023657751)
XLA Ops:
  0.6 94.0 %shard_map.94 = (bf16[128,8192]{1,0:T(8,128)(2,1)S(1)}, bf16[128,1024]{1,0:T(8,128)(2,1)S(1)}, bf16[128,1024]{1,0:T(8,128)(2,1)S(1)}) custom-call(bf16[128,8192]{1,0:T(8,128)(2,1)} %q_hbm.1, bf16[128,1024]{1,0:T(8,128)(2,1)} %k_hbm.1, bf16[128,1024]{1,0:T(8,128)(2,1)} %v_hbm.1, bf16[128,8192]{1,0:T(8,128)(2,1)} %o_hbm.1, bf16[128,8192]{1,0:T(8,128)(2,1)} %d_hbm.1, ...), custom_call_target="tpu_custom_call" | custom-call | flops 10737418240 | bytes 10485760 | tf_op jit(solution)/shard_map/pallas_call | solution.py:319
  94.6 1.3 %copy.13 = bf16[128,8192]{1,0:T(8,128)(2,1)} copy(bf16[128,8192]{1,0:T(8,128)(2,1)S(1)} %get-tuple-element.3) | data formatting | bytes 4194304
  96.0 0.7 copy.14
  96.7 0.7 copy.15
